TPU v7x, 256 devices: a whole 4x4x8 slice. The times are simulated.
256 devices in a mesh: shot: 4 (over z_lo), rr: 4 (over x), rc: 16 (over y, z_hi, core).
Axes of the slice: x: 4, y: 4, z: 8 (z_hi: 2, z_lo: 4; z = z_hi * 4 + z_lo), core: 2. Of those that a mesh axis runs over, the one named last changes fastest.
Arguments:
- records: bfloat16 [2, 8192, 4096], P(None, ('rr', 'rc'), 'shot'), may hold values from -0.44194174 to 0.44194174
Outputs:
- point_spread: float32 [2, 4, 16, 4, 32, 4, 2048], P(None, 'rr', None, 'shot', None, None, 'rc')
All inputs are finite; a program needn't handle non-finite values.
Results may differ from a plain program's by a relative error of at most 0.0003.
Values may be sent and summed in bfloat16 or wider, within the bound.
A program may use at most 128 MiB of HBM per device.

v0:
```python
import jax
import jax.numpy as jnp
from jax import lax
from jax.sharding import PartitionSpec as P


def complex_rows(segment):
    return jnp.stack([segment, jnp.stack([segment[1], -segment[0]])])


def tile_rows(segment, columns):
    stacked = complex_rows(segment)
    return jnp.einsum("xynt,ymt->xnm", stacked, columns, preferred_element_type=jnp.float32)


def on_device(records):
    strips = lax.axis_size("rc")
    blocks = lax.axis_size("rr")
    groups = lax.axis_size("shot")
    strip_rows = records.shape[1]
    sub_rows = strip_rows // groups
    columns = lax.all_gather(records, "rr", axis=1, tiled=True)
    partial_tile = tile_rows(lax.all_gather(records, "rc", axis=1, tiled=True), columns)
    shaped = partial_tile.reshape(2, strips, groups, sub_rows, blocks, strip_rows)
    summed = lax.psum_scatter(shaped, "shot", scatter_dimension=2, tiled=True)
    point_spread = summed.reshape(2, 1, strips, 1, sub_rows, blocks, strip_rows)
    return point_spread


def solution(mesh):
    return jax.shard_map(
        on_device,
        mesh=mesh,
        in_specs=(P(None, ("rr", "rc"), "shot"),),
        out_specs=P(None, "rr", None, "shot", None, None, "rc"),
        check_vma=False,
    )
```

profile of v0, /device:TPU:16, one launch (start us, length us, event | category | flops | bytes accessed | tf_op | source)
XLA Modules:
  0.0 345.0 jit_solution(17746245018105567188)
XLA Ops:
  6.5 0.0 all-gather.3.cloned.1.call-start
  6.5 0.7 all-gather.3.cloned.1.call-update
  7.3 0.0 all-gather.5.cloned.1.call-start
  7.3 0.7 all-gather.5.cloned.1.call-update
  8.0 0.0 reduce-scatter.2.cloned.1.call-start
  8.1 111.6 %all-gather.3.cloned.1.call-done = bf16[2,2048,1024]{2,1,0:T(8,128)(2,1)} async-done(((bf16[2,128,1024]{2,1,0:T(8,128)(2,1)}), bf16[2,2048,1024]{2,1,0:T(8,128)(2,1)}) %all-gather.3.cloned.1.call-update) | async-done | bytes 8388624 | tf_op jit(solution)/shard_map/all_gather | solution.py:23
  119.6 5.0 %fusion.9 = (bf16[1,2048,1024]{2,1,0:T(8,128)(2,1)S(1)}, bf16[1,2048,1024]{2,1,0:T(8,128)(2,1)}) fusion(bf16[2,2048,1024]{2,1,0:T(8,128)(2,1)} %all-gather.3.cloned.1.call-done), kind=kLoop, calls=%fused_computation.9 | loop fusion | flops 2097152 | bytes 16777216 | tf_op jit(solution)/shard_map/slice | solution.py:8
  124.7 6.2 %maximum_bitcast_fusion = bf16[1,2,2048,1024]{3,2,1,0:T(8,128)(2,1)} fusion(bf16[1,2048,1024]{2,1,0:T(8,128)(2,1)} %get-tuple-element.6, bf16[1,2048,1024]{2,1,0:T(8,128)(2,1)S(1)} %get-tuple-element.5), kind=kLoop, calls=%fused_computation.4 | loop fusion | flops 4194304 | bytes 16777216 | tf_op jit(solution)/shard_map/stack | solution.py:8
  130.9 20.0 %all-gather.5.cloned.1.call-done = bf16[2,512,1024]{2,1,0:T(8,128)(2,1)} async-done(((bf16[2,128,1024]{2,1,0:T(8,128)(2,1)}), bf16[2,512,1024]{2,1,0:T(8,128)(2,1)}) %all-gather.5.cloned.1.call-update) | async-done | bytes 2097168 | tf_op jit(solution)/shard_map/all_gather | solution.py:22
  151.0 15.2 %fusion.4 = f32[2,2048,512]{2,1,0:T(8,128)} fusion(bf16[1,2,2048,1024]{3,2,1,0:T(8,128)(2,1)} %maximum_bitcast_fusion, bf16[1,2,2048,1024]{3,2,1,0:T(8,128)(2,1)} %bitcast.10, bf16[2,512,1024]{2,1,0:T(8,128)(2,1)} %all-gather.5.cloned.1.call-done), kind=kOutput, calls=%fused_computation.5 | convolution fusion | flops 8598323200 | bytes 27262976 | tf_op jit(solution)/shard_map/xynt,ymt->xnm/dot_general | solution.py:13
  166.2 9.9 %reshape.6 = f32[2,16,4,32,4,128]{5,4,3,2,1,0:T(4,128)} reshape(f32[2,2048,512]{2,1,0:T(8,128)} %fusion.4) | data formatting | bytes 16777216 | tf_op jit(solution)/shard_map/reshape | solution.py:24
  176.1 7.8 %copy.3 = f32[2,16,4,32,4,128]{5,3,4,1,0,2:T(8,128)} copy(f32[2,16,4,32,4,128]{5,4,3,2,1,0:T(4,128)} %reshape.6) | data formatting | bytes 16777216 | tf_op jit(solution)/shard_map/reshape | solution.py:24
  183.8 0.0 reduce-scatter.2.cloned.1.call-update
  183.8 150.0 %reduce-scatter.2.cloned.1.call-done = f32[2,16,1,32,4,128]{5,3,4,1,0,2:T(8,128)} async-done(((f32[2,16,4,32,4,128]{5,3,4,1,0,2:T(8,128)}), f32[2,16,1,32,4,128]{5,3,4,1,0,2:T(8,128)}) %reduce-scatter.2.cloned.1.call-update) | async-done | bytes 2097168 | tf_op jit(solution)/shard_map/reduce_scatter | solution.py:25
  333.8 4.7 %copy.4 = f32[2,1,16,1,32,4,128]{6,5,4,3,2,1,0:T(4,128)} copy(f32[2,1,16,1,32,4,128]{6,4,5,2,0,3,1:T(8,128)} %bitcast.11) | data formatting | bytes 4194304 | tf_op jit(solution)/shard_map/reshape | solution.py:26
Async XLA Ops:
  6.5 113.1 %all-gather.3.cloned.1.call-start = ((), (), s32[]{:S(2)}) async-start(), calls=%async_computation.1 | async-start | bytes 8912896 | tf_op jit(solution)/shard_map/all_gather | solution.py:23
  7.3 143.7 %all-gather.5.cloned.1.call-start = ((), (), s32[]{:S(2)}) async-start(), calls=%async_computation.2 | async-start | bytes 2621440 | tf_op jit(solution)/shard_map/all_gather | solution.py:22
  8.0 325.8 %reduce-scatter.2.cloned.1.call-start = ((), (), s32[]{:S(2)}) async-start(), calls=%async_computation.3 | async-start | bytes 10485760 | tf_op jit(solution)/shard_map/reduce_scatter | solution.py:25
Sparse Core Ops, SparseCore 0:
  10.1 109.4 all-gather.2
  121.4 29.4 all-gather.4
  184.0 149.8 reduce-scatter.1
where the time goes:
time: 346 us; the launch traced here: 345 us
  waiting for transfers between devices  283 us (82%)
  local copies, waits for them, and re-layouts  22.3 us (6%)
  matrix products  15.2 us (4%)
  between operations  13.1 us (4%)
  other arithmetic  11.3 us (3%)
    reduce_scatter x1, waiting for transfers between devices, on_device(): summed = lax.psum_scatter(shaped, 'shot', scatter_dimension=2, tiled=True)  150 us
    all_gather x1, waiting for transfers between devices, on_device(): lax.all_gather(records, 'rc', axis=1, tiled=True)  112 us
    all_gather x1, waiting for transfers between devices, on_device(): columns = lax.all_gather(records, 'rr', axis=1, tiled=True)  20 us
    reshape x2, local copies, waits for them, and re-layouts, on_device(): partial_tile.reshape(2, strips, groups, sub_rows, blocks, strip_rows)  17.7 us
    dot_general x1, matrix products, tile_rows(): jnp.einsum('xynt,ymt->xnm', stacked, columns, preferred_element_type=jnp....  15.2 us
  transfers between devices with their start and end apart: 3, of which 3 were waited for; matrix products, arithmetic and copies ran while one was open for 3% of the time, Pallas kernels for 0%

commit v1 on v0

v1 whole, which is shorter than its diff:
```python
import jax
import jax.numpy as jnp
from jax import lax
from jax.experimental import pallas as pl
from jax.experimental.pallas import tpu as pltpu
from jax.sharding import PartitionSpec as P

MESH = pl.DeviceIdType.MESH
NT = (((1,), (1,)), ((), ()))
ROWS, SHOTS = 128, 1024
SUB = 32
PEAK = 1024.0
TINY = 1e-34
N_SEMS = 120


def kernel(x_ref, o_ref, cols, rows, w, acc0, acc1, enc_out, enc_in, top_out, top_in, ssem, rsem, lsem):
    zlo = lax.axis_index("shot")
    x = lax.axis_index("rr")
    rc = lax.axis_index("rc")
    y = rc // 4
    zhi = (rc // 2) % 2
    c = rc % 2

    def dev(x, y, zhi, zlo, c):
        return {"shot": zlo, "rr": x, "rc": y * 4 + zhi * 2 + c}

    q_odd = zlo + 1 - 2 * (zlo % 2)
    q_two = (zlo + 2) % 4
    q_three = 3 - zlo
    xs = {0: x, 1: (x + 1) % 4, -1: (x + 3) % 4, 2: (x + 2) % 4}
    ys = {0: y, 1: (y + 1) % 4, -1: (y + 3) % 4, 2: (y + 2) % 4}
    xdev = {s: dev(xs[s], y, zhi, zlo, c) for s in (1, -1)}
    ydev = {s: dev(x, ys[s], zhi, zlo, c) for s in (1, -1)}
    shot_pair = dev(x, y, zhi, q_two, c)
    other_half = dev(x, y, 1 - zhi, q_two, c)
    sum_pair = dev(x, y, zhi, q_odd, c)
    sibling = dev(x, y, zhi, zlo, 1 - c)
    partners = [xdev[1], xdev[-1], ydev[1], ydev[-1], shot_pair, other_half, sum_pair, sibling]

    barrier = pltpu.get_barrier_semaphore()
    for p in partners:
        pl.semaphore_signal(barrier, inc=1, device_id=p, device_id_type=MESH)
    pl.semaphore_wait(barrier, len(partners))

    msgs = {}

    def send(key, src, dst, to):
        i = len(msgs)
        copy = pltpu.make_async_remote_copy(
            src_ref=src, dst_ref=dst, send_sem=ssem.at[i], recv_sem=rsem.at[i], device_id=to, device_id_type=MESH
        )
        copy.start()
        msgs[key] = copy

    def got(*keys):
        for key in keys:
            msgs[key].wait_recv()

    locals_ = []

    def local(src, dst):
        copy = pltpu.make_async_copy(src, dst, lsem.at[len(locals_)])
        copy.start()
        locals_.append(copy)

    def part(q):
        return pl.ds(pl.multiple_of(q * SUB, SUB), SUB)

    def strip(zown, yy):
        half = zhi if zown else 1 - zhi
        return ys[yy] * 4 + half * 2 + c

    row_part = {0: q_odd, 1: zlo}
    there_part = {0: q_three, 1: q_two}

    def y_send(zown, g, q, src=None):
        spot = rows.at[q, g, :, strip(zown, 0)]
        src = spot if src is None else src
        for s in (1, -1):
            send(("yd", zown, g, q, s), src, spot, ydev[s])
        send(("cc", zown, g, q, 0), src, spot, sibling)

    def y_forward(zown, g, q):
        for s in (1, -1):
            got(("yd", zown, g, q, s))
            p = 0 if s == 1 else 1
            spot = rows.at[q, g, p, strip(zown, -s)]
            send(("yf", zown, g, q, s), spot, spot, ydev[s])
        for s in (1, -1):
            spot = rows.at[q, g, :, strip(zown, s)]
            send(("cc", zown, g, q, s), spot, spot, sibling)

    def y_last(zown, g, q):
        got(("yf", zown, g, q, 1), ("yf", zown, g, q, -1))
        spot = rows.at[q, g, :, strip(zown, 2)]
        send(("cc", zown, g, q, 2), spot, spot, sibling)

    order = [q_odd, q_three, q_two, zlo]
    sent_as = [q_three, q_odd, zlo, q_two]

    def x_send(i):
        spot = cols.at[x, 1, :, part(order[i])]
        for s in (1, -1):
            send(("xd", 1, s, i), spot, spot, xdev[s])

    def x_forward(i):
        for s in (1, -1):
            got(("xd", 1, s, i))
            p = 0 if s == 1 else 1
            spot = cols.at[xs[-s], 1, p, part(order[i])]
            send(("xf", 1, s, i), spot, spot, xdev[s])

    for i in range(2):
        send(("l2", i), x_ref.at[:, part(sent_as[i])], cols.at[x, 1, :, part(sent_as[i])], shot_pair)
    send(("zo", 0), x_ref.at[:, part(there_part[0])], rows.at[0, 1, :, strip(True, 0)], other_half)
    y_send(True, 0, 0, x_ref.at[:, part(row_part[0])])
    for s in (1, -1):
        send(("xd", 0, s), x_ref, cols.at[x, 0], xdev[s])
    for i in range(2, 4):
        send(("l2", i), x_ref.at[:, part(sent_as[i])], cols.at[x, 1, :, part(sent_as[i])], shot_pair)
    send(("zo", 1), x_ref.at[:, part(there_part[1])], rows.at[1, 1, :, strip(True, 0)], other_half)
    y_send(True, 0, 1, x_ref.at[:, part(row_part[1])])
    local(x_ref.at[:, part(row_part[0])], rows.at[0, 0, :, strip(True, 0)])
    local(x_ref.at[:, part(row_part[1])], rows.at[1, 0, :, strip(True, 0)])

    def build(d, g, real, imag):
        w[d, g, 0, 0:ROWS] = real
        w[d, g, 0, ROWS:] = -imag
        w[d, g, 1, 0:ROWS] = imag
        w[d, g, 1, ROWS:] = real

    def build_from(d, g, xi):
        build(d, g, cols[xi, g, 0], cols[xi, g, 1])

    build(0, 0, x_ref[0], x_ref[1])

    y_forward(True, 0, 0)
    got(("zo", 0))
    y_send(False, 1, 0)
    got(("l2", 0))
    y_send(True, 1, 0, cols.at[x, 1, :, part(row_part[0])])
    local(cols.at[x, 1, :, part(row_part[0])], rows.at[0, 1, :, strip(True, 0)])
    x_send(0)
    y_forward(True, 0, 1)
    y_forward(False, 1, 0)
    got(("l2", 1))
    send(("zr", 0), cols.at[x, 1, :, part(there_part[0])], rows.at[0, 0, :, strip(True, 0)], other_half)
    x_send(1)
    got(("zo", 1))
    y_send(False, 1, 1)
    y_forward(True, 1, 0)
    for s in (1, -1):
        got(("xd", 0, s))
        p = 0 if s == 1 else 1
        spot = cols.at[xs[-s], 0, p]
        send(("xf", 0, s), spot, spot, xdev[s])
    y_last(True, 0, 0)
    y_last(True, 0, 1)
    y_last(False, 1, 0)
    y_last(True, 1, 0)
    y_forward(False, 1, 1)
    got(("zr", 0))
    y_send(False, 0, 0)
    got(("l2", 2))
    send(("zr", 1), cols.at[x, 1, :, part(there_part[1])], rows.at[1, 0, :, strip(True, 0)], other_half)
    x_send(2)
    x_forward(0)
    x_forward(1)
    y_forward(False, 0, 0)
    got(("l2", 3))
    y_send(True, 1, 1, cols.at[x, 1, :, part(row_part[1])])
    local(cols.at[x, 1, :, part(row_part[1])], rows.at[1, 1, :, strip(True, 0)])
    x_send(3)
    build_from(0, 1, x)
    y_last(False, 0, 0)
    got(("zr", 1))
    y_send(False, 0, 1)

    def take_sibling(q):
        for zown in (True, False):
            for g in (0, 1):
                for yy in (0, 1, -1, 2):
                    got(("cc", zown, g, q, yy))

    def product(q, d):
        total = None
        for g in (0, 1):
            for p in (0, 1):
                left = rows[q, g, p].reshape(16 * SUB, SHOTS)
                term = lax.dot_general(left, w[d, g, p], NT, preferred_element_type=jnp.float32)
                total = term if total is None else total + term
        return total

    def give(d):
        acc0[...] = product(0, d)

        def look(r, top):
            return jnp.maximum(top, jnp.abs(acc0[pl.ds(r * 64, 64)]).reshape(8, 8, 256).max(axis=0))

        top = lax.fori_loop(0, 8, look, jnp.zeros((8, 256), jnp.float32)).max(axis=0, keepdims=True)
        top = jnp.maximum(top, TINY)
        top_out[d] = jnp.broadcast_to(top, (8, 256))
        scale = PEAK / top

        def code(r, _):
            at = pl.ds(pl.multiple_of(r * 64, 64), 64)
            t = acc0[at] * scale
            t2 = t * t
            t4 = t2 * t2
            t12 = t4 * t4 * t4
            enc_out[d, at] = jnp.where(t < 0, -t12, t12).astype(jnp.bfloat16)
            return 0

        lax.fori_loop(0, 8, code, 0)
        send(("ev", d), enc_out.at[d], enc_in.at[d], sum_pair)
        send(("et", d), top_out.at[d], top_in.at[d], sum_pair)

    for copy in locals_[:3]:
        copy.wait()
    take_sibling(0)
    give(0)

    y_last(False, 1, 1)
    y_forward(True, 1, 1)
    x_forward(2)
    y_forward(False, 0, 1)
    x_forward(3)
    build_from(1, 0, xs[1])
    build_from(1, 1, xs[1])
    give(1)
    y_last(True, 1, 1)
    y_last(False, 0, 1)
    build_from(2, 0, xs[-1])
    build_from(2, 1, xs[-1])
    give(2)
    for s in (1, -1):
        got(("xf", 0, s))
        for i in range(4):
            got(("xf", 1, s, i))
    build_from(3, 0, xs[2])
    build_from(3, 1, xs[2])
    give(3)

    locals_[3].wait()
    take_sibling(1)

    def keep(d, _):
        acc1[d] = product(1, d)
        return 0

    lax.fori_loop(0, 4, keep, 0)

    for d, xi in enumerate((xs[0], xs[1], xs[-1], xs[2])):
        got(("ev", d), ("et", d))
        top = top_in[d][0:1] * (1.0 / PEAK)

        def finish(r, _):
            at = pl.ds(pl.multiple_of(r * 64, 64), 64)
            u = enc_in[d, at].astype(jnp.float32)
            size = jnp.exp2(jnp.log2(jnp.abs(u)) * (1.0 / 12.0)) * top
            total = acc1[d, at] + jnp.where(u < 0, -size, size)
            for k in (0, 1):
                o_ref[pl.ds(k * 2048 + r * 256 + xi, 64, stride=4), :] = total[:, k * ROWS : (k + 1) * ROWS]
            return 0

        lax.fori_loop(0, 8, finish, 0)

    for copy in msgs.values():
        copy.wait_send()


def on_device(records):
    flat = pl.pallas_call(
        kernel,
        out_shape=jax.ShapeDtypeStruct((4096, 128), jnp.float32),
        in_specs=[pl.BlockSpec(memory_space=pltpu.VMEM)],
        out_specs=pl.BlockSpec(memory_space=pltpu.VMEM),
        scratch_shapes=[
            pltpu.VMEM((4, 2, 2, ROWS, SHOTS), jnp.bfloat16),
            pltpu.VMEM((2, 2, 2, 16, SUB, SHOTS), jnp.bfloat16),
            pltpu.VMEM((4, 2, 2, 2 * ROWS, SHOTS), jnp.bfloat16),
            pltpu.VMEM((512, 256), jnp.float32),
            pltpu.VMEM((4, 512, 256), jnp.float32),
            pltpu.VMEM((4, 512, 256), jnp.bfloat16),
            pltpu.VMEM((4, 512, 256), jnp.bfloat16),
            pltpu.VMEM((4, 8, 256), jnp.float32),
            pltpu.VMEM((4, 8, 256), jnp.float32),
            pltpu.SemaphoreType.DMA((N_SEMS,)),
            pltpu.SemaphoreType.DMA((N_SEMS,)),
            pltpu.SemaphoreType.DMA((4,)),
        ],
        compiler_params=pltpu.CompilerParams(
            collective_id=0, has_side_effects=True, vmem_limit_bytes=52 * 2**20
        ),
        cost_estimate=pl.CostEstimate(flops=8_600_000_000, bytes_accessed=3_000_000, transcendentals=1_000_000),
    )(records)
    return flat.reshape(2, 1, 16, 1, 32, 4, 128)


def solution(mesh):
    return jax.shard_map(
        on_device,
        mesh=mesh,
        in_specs=(P(None, ("rr", "rc"), "shot"),),
        out_specs=P(None, "rr", None, "shot", None, None, "rc"),
        check_vma=False,
    )
```

time: 346 us -> 80.1 us (0.23)
  the two profiles are of different devices: /device:TPU:16 before, /device:TPU:1 now
where the time goes in v1:
time: 80.1 us; the launch traced here: 80 us
  Pallas kernels  75.8 us (95%)
  local copies, waits for them, and re-layouts  4.18 us (5%)
    pallas_call x1, Pallas kernels, on_device(): pl.pallas_call(kernel, out_shape=jax.ShapeDtypeStruct((4096, 128), jnp.fl...  75.8 us
    unnamed x3, local copies, waits for them, and re-layouts  4.18 us

profile of v1, /device:TPU:1, one launch (start us, length us, event | category | flops | bytes accessed | tf_op | source)
XLA Modules:
  0.0 80.0 jit_solution(13511116113140920852)
XLA Ops:
  0.0 0.0 copy-start
  0.0 1.0 %copy-done = bf16[2,128,1024]{2,1,0:T(8,128)(2,1)S(1)} copy-done((bf16[2,128,1024]{2,1,0:T(8,128)(2,1)S(1)}, bf16[2,128,1024]{2,1,0:T(8,128)(2,1)}, u32[]{:S(2)}) %copy-start) | copy-done | bytes 524312
  1.0 75.8 %shard_map.17 = f32[4096,128]{1,0:T(8,128)} custom-call(bf16[2,128,1024]{2,1,0:T(8,128)(2,1)S(1)} %copy-done), custom_call_target="tpu_custom_call" | custom-call | flops 8600000512 | bytes 3000000 | tf_op jit(solution)/shard_map/pallas_call | solution.py:274
  76.9 3.1 %copy.4 = f32[2,1,16,1,32,4,128]{6,5,4,3,2,1,0:T(4,128)} copy(f32[2,1,16,1,32,4,128]{6,5,4,3,2,1,0:T(4,128)} %bitcast.3) | data formatting | bytes 4194304
Async XLA Ops:
  0.0 1.0 %copy-start = (bf16[2,128,1024]{2,1,0:T(8,128)(2,1)S(1)}, bf16[2,128,1024]{2,1,0:T(8,128)(2,1)}, u32[]{:S(2)}) copy-start(bf16[2,128,1024]{2,1,0:T(8,128)(2,1)} %x_ref.1) | copy-start | bytes 1572868

commit v2 on v0

v2 whole, which is shorter than its diff:
```python
import jax
import jax.numpy as jnp
from jax import lax
from jax.experimental import pallas as pl
from jax.experimental.pallas import tpu as pltpu
from jax.sharding import PartitionSpec as P

MESH = pl.DeviceIdType.MESH
NT = (((1,), (1,)), ((), ()))
ROWS, SHOTS = 128, 1024
SUB = 32
HALF = 8 * SUB
WIDE = 2 * ROWS
PEAK = 512.0
TINY = 1e-34
N_SEMS = 108
EV, ET = 92, 100


def kernel(x_ref, o_ref, cols, rows, w, acc0, acc1, enc_out, enc_in, top_out, top_in, ssem, rsem, lsem):
    zlo = lax.axis_index("shot")
    x = lax.axis_index("rr")
    rc = lax.axis_index("rc")
    y = rc // 4
    zhi = (rc // 2) % 2
    c = rc % 2

    def dev(x, y, zhi, zlo, c):
        return {"shot": zlo, "rr": x, "rc": y * 4 + zhi * 2 + c}

    q_odd = zlo + 1 - 2 * (zlo % 2)
    q_two = (zlo + 2) % 4
    q_three = 3 - zlo
    xs = {0: x, 1: (x + 1) % 4, -1: (x + 3) % 4, 2: (x + 2) % 4}
    ys = {0: y, 1: (y + 1) % 4, -1: (y + 3) % 4, 2: (y + 2) % 4}
    xdev = {s: dev(xs[s], y, zhi, zlo, c) for s in (1, -1)}
    ydev = {s: dev(x, ys[s], zhi, zlo, c) for s in (1, -1)}
    shot_pair = dev(x, y, zhi, q_two, c)
    other_half = dev(x, y, 1 - zhi, q_two, c)
    sum_pair = dev(x, y, zhi, q_odd, c)
    sibling = dev(x, y, zhi, zlo, 1 - c)
    partners = [xdev[1], xdev[-1], ydev[1], ydev[-1], shot_pair, other_half, sum_pair, sibling]

    barrier = pltpu.get_barrier_semaphore()
    for p in partners:
        pl.semaphore_signal(barrier, inc=1, device_id=p, device_id_type=MESH)
    pl.semaphore_wait(barrier, len(partners))

    msgs = {}

    def plan(key, src, dst, to):
        i = len(msgs)
        msgs[key] = pltpu.make_async_remote_copy(
            src_ref=src, dst_ref=dst, send_sem=ssem.at[i], recv_sem=rsem.at[i], device_id=to, device_id_type=MESH
        )

    def go(*keys):
        for key in keys:
            msgs[key].start()

    def got(*keys):
        for key in keys:
            msgs[key].wait_recv()

    def part(q):
        return pl.ds(pl.multiple_of(q * SUB, SUB), SUB)

    def strip(zown, yy):
        half = zhi if zown else 1 - zhi
        return half * 8 + ys[yy] * 2 + c

    row_part = (q_odd, zlo)
    there_part = (q_three, q_two)
    order = (q_three, q_odd, q_two, zlo)
    sent_as = (q_odd, q_three, zlo, q_two)
    here = strip(True, 0)

    for i in range(4):
        plan(("l2", i), x_ref.at[:, part(sent_as[i])], cols.at[x, 1, :, part(sent_as[i])], shot_pair)
    for q in (0, 1):
        plan(("zo", q), x_ref.at[:, part(there_part[q])], rows.at[q, 1, :, here], other_half)
        plan(("zr", q), cols.at[x, 1, :, part(there_part[q])], rows.at[q, 0, :, here], other_half)
    for s in (1, -1):
        p = 0 if s == 1 else 1
        plan(("xd", 0, s, 0), x_ref, cols.at[x, 0], xdev[s])
        spot = cols.at[xs[-s], 0, p]
        plan(("xf", 0, s, 0), spot, spot, xdev[s])
        for i in range(4):
            spot = cols.at[x, 1, :, part(order[i])]
            plan(("xd", 1, s, i), spot, spot, xdev[s])
            spot = cols.at[xs[-s], 1, p, part(order[i])]
            plan(("xf", 1, s, i), spot, spot, xdev[s])
    for zown in (True, False):
        for g in (0, 1):
            for q in (0, 1):
                spot = rows.at[q, g, :, strip(zown, 0)]
                src = spot
                if zown:
                    src = x_ref.at[:, part(row_part[q])] if g == 0 else cols.at[x, 1, :, part(row_part[q])]
                for s in (1, -1):
                    p = 0 if s == 1 else 1
                    plan(("yd", zown, g, q, s), src, spot, ydev[s])
                    forward = rows.at[q, g, p, strip(zown, -s)]
                    plan(("yf", zown, g, q, s), forward, forward, ydev[s])
                plan(("cc", zown, g, q, 0), src, spot, sibling)
                for yy in (1, -1, 2):
                    spot = rows.at[q, g, :, strip(zown, yy)]
                    plan(("cc", zown, g, q, yy), spot, spot, sibling)

    own = {
        (g, q): pltpu.make_async_copy(
            x_ref.at[:, part(row_part[q])] if g == 0 else cols.at[x, 1, :, part(row_part[q])],
            rows.at[q, g, :, here],
            lsem.at[g * 2 + q],
        )
        for g in (0, 1)
        for q in (0, 1)
    }

    def y_send(zown, g, q):
        go(("yd", zown, g, q, 1), ("yd", zown, g, q, -1), ("cc", zown, g, q, 0))

    def y_forward(zown, g, q):
        for s in (1, -1):
            got(("yd", zown, g, q, s))
            go(("yf", zown, g, q, s))
        go(("cc", zown, g, q, 1), ("cc", zown, g, q, -1))

    def y_last(zown, g, q):
        got(("yf", zown, g, q, 1), ("yf", zown, g, q, -1))
        go(("cc", zown, g, q, 2))

    def x_send(g, i):
        go(("xd", g, 1, i), ("xd", g, -1, i))

    def x_forward(g, i):
        for s in (1, -1):
            got(("xd", g, s, i))
            go(("xf", g, s, i))

    def build(d, g, real, imag):
        w[d, g, 0, 0:ROWS] = real
        w[d, g, 0, ROWS:] = -imag
        w[d, g, 1, 0:ROWS] = imag
        w[d, g, 1, ROWS:] = real

    def build_from(d, g, xi):
        build(d, g, cols[xi, g, 0], cols[xi, g, 1])

    def take_sibling(zown, q):
        for g in (0, 1):
            for yy in (0, 1, -1, 2):
                got(("cc", zown, g, q, yy))

    go(("l2", 0), ("l2", 1), ("zo", 0))
    y_send(True, 0, 0)
    x_send(0, 0)
    go(("l2", 2), ("l2", 3), ("zo", 1))
    y_send(True, 0, 1)
    own[0, 0].start()
    own[0, 1].start()
    build(0, 0, x_ref[0], x_ref[1])

    y_forward(True, 0, 0)
    got(("zo", 0))
    y_send(False, 1, 0)
    got(("l2", 0))
    go(("zr", 0))
    x_send(1, 0)
    y_forward(False, 1, 0)
    y_last(True, 0, 0)
    got(("l2", 1))
    y_send(True, 1, 0)
    own[1, 0].start()
    x_send(1, 1)
    got(("zr", 0))
    y_send(False, 0, 0)
    x_forward(0, 0)
    y_last(False, 1, 0)
    y_forward(True, 1, 0)
    build_from(1, 0, xs[1])
    got(("l2", 2))
    go(("zr", 1))
    x_send(1, 2)
    y_forward(False, 0, 0)
    y_forward(True, 0, 1)
    got(("zo", 1))
    y_send(False, 1, 1)
    y_last(True, 1, 0)
    x_forward(1, 0)
    x_forward(1, 1)
    y_last(False, 0, 0)
    build_from(2, 0, xs[-1])
    got(("l2", 3))
    y_send(True, 1, 1)
    own[1, 1].start()
    x_send(1, 3)
    build_from(0, 1, x)
    y_last(True, 0, 1)
    got(("zr", 1))
    y_send(False, 0, 1)
    own[0, 0].wait()
    own[1, 0].wait()
    take_sibling(True, 0)

    def before_1():
        take_sibling(False, 0)
        y_forward(False, 1, 1)

    def before_2():
        y_forward(True, 1, 1)
        x_forward(1, 2)
        x_forward(1, 3)
        build_from(1, 1, xs[1])

    def before_3():
        y_forward(False, 0, 1)
        y_last(False, 1, 1)

    def before_4():
        y_last(True, 1, 1)
        build_from(2, 1, xs[-1])

    def before_5():
        y_last(False, 0, 1)

    def before_6():
        for s in (1, -1):
            got(("xf", 0, s, 0))
            for i in range(4):
                got(("xf", 1, s, i))
        build_from(3, 0, xs[2])
        build_from(3, 1, xs[2])

    def product(left, d):
        total = None
        for g in (0, 1):
            for p in (0, 1):
                term = lax.dot_general(left(g, p), w[d, g, p], NT, preferred_element_type=jnp.float32)
                total = term if total is None else total + term
        return total

    def sums(i):
        copies = []
        for a, b, first in ((enc_out, enc_in, EV), (top_out, top_in, ET)):
            copies.append(
                pltpu.make_async_remote_copy(
                    src_ref=a.at[i],
                    dst_ref=b.at[i],
                    send_sem=ssem.at[first + i],
                    recv_sem=rsem.at[first + i],
                    device_id=sum_pair,
                    device_id_type=MESH,
                )
            )
        return copies

    def give(i, _):
        for k, block in ((1, before_1), (2, before_2), (3, before_3), (4, before_4), (5, before_5), (6, before_6)):
            pl.when(i == k)(block)
        d = i // 2
        half = jnp.where(i % 2 == 0, zhi, 1 - zhi)
        at = pl.ds(half * 8, 8)
        acc0[...] = product(lambda g, p: rows[0, g, p, at].reshape(HALF, SHOTS), d)

        def look(r, top):
            return jnp.maximum(top, jnp.abs(acc0[pl.ds(pl.multiple_of(r * 64, 64), 64)]).reshape(8, 8, WIDE).max(axis=0))

        top = lax.fori_loop(0, 4, look, jnp.zeros((8, WIDE), jnp.float32)).max(axis=0, keepdims=True)
        top = jnp.maximum(top, TINY)
        top_out[i] = jnp.broadcast_to(top, (8, WIDE))
        scale = PEAK / top

        def code(r, _):
            at = pl.ds(pl.multiple_of(r * 64, 64), 64)
            t = acc0[at] * scale
            t2 = t * t
            t4 = t2 * t2
            power = t4 * t4 * t4 * t2
            enc_out[i, at] = jnp.where(t < 0, -power, power).astype(jnp.bfloat16)
            return 0

        lax.fori_loop(0, 4, code, 0)
        for copy in sums(i):
            copy.start()
        return 0

    lax.fori_loop(0, 8, give, 0)

    own[0, 1].wait()
    own[1, 1].wait()
    take_sibling(True, 1)
    take_sibling(False, 1)

    def keep(d, _):
        acc1[d] = product(lambda g, p: rows[1, g, p].reshape(2 * HALF, SHOTS), d)
        return 0

    lax.fori_loop(0, 4, keep, 0)

    def finish(i, _):
        for copy in sums(i):
            copy.wait_recv()
        d = i // 2
        half = jnp.where(i % 2 == 0, zhi, 1 - zhi)
        xi = (x + d + (d // 2) * (1 - 2 * (d % 2))) % 4
        top = top_in[i][0:1] * (1.0 / PEAK)

        def add(r, _):
            u = enc_in[i, pl.ds(pl.multiple_of(r * 64, 64), 64)].astype(jnp.float32)
            size = jnp.exp2(jnp.log2(jnp.abs(u)) * (1.0 / 14.0)) * top
            at = pl.ds(pl.multiple_of(half * HALF + r * 64, 64), 64)
            total = acc1[d, at] + jnp.where(u < 0, -size, size)
            for k in (0, 1):
                o_ref[pl.ds(k * 2048 + r * 512 + half * 256 + xi, 64, stride=4), :] = total[:, k * ROWS : (k + 1) * ROWS]
            return 0

        lax.fori_loop(0, 4, add, 0)
        return 0

    lax.fori_loop(0, 8, finish, 0)

    for copy in msgs.values():
        copy.wait_send()

    def drain(i, _):
        for copy in sums(i):
            copy.wait_send()
        return 0

    lax.fori_loop(0, 8, drain, 0)


def on_device(records):
    flat = pl.pallas_call(
        kernel,
        out_shape=pltpu.VMEM((4096, 128), jnp.float32),
        in_specs=[pl.BlockSpec(memory_space=pltpu.VMEM)],
        out_specs=pl.BlockSpec(memory_space=pltpu.VMEM),
        scratch_shapes=[
            pltpu.VMEM((4, 2, 2, ROWS, SHOTS), jnp.bfloat16),
            pltpu.VMEM((2, 2, 2, 16, SUB, SHOTS), jnp.bfloat16),
            pltpu.VMEM((4, 2, 2, WIDE, SHOTS), jnp.bfloat16),
            pltpu.VMEM((HALF, WIDE), jnp.float32),
            pltpu.VMEM((4, 2 * HALF, WIDE), jnp.float32),
            pltpu.VMEM((8, HALF, WIDE), jnp.bfloat16),
            pltpu.VMEM((8, HALF, WIDE), jnp.bfloat16),
            pltpu.VMEM((8, 8, WIDE), jnp.float32),
            pltpu.VMEM((8, 8, WIDE), jnp.float32),
            pltpu.SemaphoreType.DMA((N_SEMS,)),
            pltpu.SemaphoreType.DMA((N_SEMS,)),
            pltpu.SemaphoreType.DMA((4,)),
        ],
        compiler_params=pltpu.CompilerParams(
            collective_id=0, has_side_effects=True, vmem_limit_bytes=52 * 2**20
        ),
        cost_estimate=pl.CostEstimate(flops=8_600_000_000, bytes_accessed=3_000_000, transcendentals=1_000_000),
    )(records)
    return flat.reshape(2, 1, 16, 1, 32, 4, 128)


def solution(mesh):
    return jax.shard_map(
        on_device,
        mesh=mesh,
        in_specs=(P(None, ("rr", "rc"), "shot"),),
        out_specs=P(None, "rr", None, "shot", None, None, "rc"),
        check_vma=False,
    )
```

time: 346 us -> 68.8 us (0.20)
  waiting for transfers between devices: 283 us -> 0 us
  Pallas kernels: 0 us -> 66.8 us
  local copies, waits for them, and re-layouts: 22.3 us -> 1.32 us
  matrix products: 15.2 us -> 0 us
  between operations: 13.1 us -> 0.01 us
  other arithmetic: 11.3 us -> 0 us
    reduce_scatter x1 -> x0, waiting for transfers between devices: 150 us -> none  [on_device(): summed = lax.psum_scatter(shaped, 'shot', scatter_dimension=2, tiled=True)]
    all_gather x2 -> x0, waiting for transfers between devices: 132 us -> none  [the longest x1 112 us: on_device(): lax.all_gather(records, 'rc', axis=1, tiled=True)]
    pallas_call x0 -> x1, Pallas kernels: none -> 66.8 us  [on_device(): pl.pallas_call(kernel, out_shape=pltpu.VMEM((4096, 128), jnp.float32), in...]
    reshape x3 -> x0, local copies, waits for them, and re-layouts: 22.3 us -> none  [the longest x2 17.7 us: on_device(): partial_tile.reshape(2, strips, groups, sub_rows, blocks, strip_rows)]
    dot_general x1 -> x0, matrix products: 15.2 us -> none  [tile_rows(): jnp.einsum('xynt,ymt->xnm', stacked, columns, preferred_element_type=jnp....]
    another operation x1 -> x0, other arithmetic: 6.24 us -> none  [complex_rows(): return jnp.stack([segment, jnp.stack([segment[1], -segment[0]])])]
    slice x1 -> x0, other arithmetic: 5.04 us -> none  [complex_rows(): return jnp.stack([segment, jnp.stack([segment[1], -segment[0]])])]
  transfers between devices with their start and end apart: 3 -> 0, of which waited for: 3 -> 0; matrix products, arithmetic and copies ran while one was open for 3% -> 0% of each run, Pallas kernels for 0% -> 0%
where the time goes in v2:
time: 68.8 us; the launch traced here: 68.1 us
  Pallas kernels  66.8 us (97%)
  local copies, waits for them, and re-layouts  1.32 us (2%)
    pallas_call x1, Pallas kernels, on_device(): pl.pallas_call(kernel, out_shape=pltpu.VMEM((4096, 128), jnp.float32), in...  66.8 us

profile of v2, /device:TPU:16, one launch (start us, length us, event | category | flops | bytes accessed | tf_op | source)
XLA Modules:
  0.0 68.1 jit_solution(7099270465289411449)
XLA Ops:
  0.0 66.8 %shard_map.17 = f32[4096,128]{1,0:T(8,128)S(1)} custom-call(bf16[2,128,1024]{2,1,0:T(8,128)(2,1)} %x_ref.1), custom_call_target="tpu_custom_call" | custom-call | flops 8600000512 | bytes 3000000 | tf_op jit(solution)/shard_map/pallas_call | solution.py:335
  66.8 1.3 %copy.4 = f32[2,1,16,1,32,4,128]{6,5,4,3,2,1,0:T(4,128)} copy(f32[2,1,16,1,32,4,128]{6,5,4,3,2,1,0:T(4,128)S(1)} %bitcast.3) | data formatting | bytes 4194304

commit v3 on v2

--- a/solution.py
+++ b/solution.py
@@ -13,11 +13,11 @@
 WIDE = 2 * ROWS
 PEAK = 512.0
 TINY = 1e-34
-N_SEMS = 108
-EV, ET = 92, 100
-
-
-def kernel(x_ref, o_ref, cols, rows, w, acc0, acc1, enc_out, enc_in, top_out, top_in, ssem, rsem, lsem):
+N_SEMS = 142
+EV, ET = 126, 134
+
+
+def kernel(x_ref, o_ref, cols, rows, w, acc0, acc1, enc_out, enc_in, top_out, top_in, ssem, rsem, lsem, ready, mine):
     zlo = lax.axis_index("shot")
     x = lax.axis_index("rr")
     rc = lax.axis_index("rc")
@@ -39,12 +39,21 @@
     other_half = dev(x, y, 1 - zhi, q_two, c)
     sum_pair = dev(x, y, zhi, q_odd, c)
     sibling = dev(x, y, zhi, zlo, 1 - c)
-    partners = [xdev[1], xdev[-1], ydev[1], ydev[-1], shot_pair, other_half, sum_pair, sibling]
+    near = [xdev[1], xdev[-1], ydev[1], ydev[-1], shot_pair, sum_pair, sibling]
 
     barrier = pltpu.get_barrier_semaphore()
-    for p in partners:
+    for p in near:
         pl.semaphore_signal(barrier, inc=1, device_id=p, device_id_type=MESH)
-    pl.semaphore_wait(barrier, len(partners))
+
+    @pl.when(zhi == 0)
+    def _():
+        pl.semaphore_signal(barrier, inc=1, device_id=other_half, device_id_type=MESH)
+
+    pl.semaphore_wait(barrier, len(near) + zhi)
+
+    @pl.when(zhi == 1)
+    def _():
+        pl.semaphore_signal(ready, inc=1, device_id=other_half, device_id_type=MESH)
 
     msgs = {}
 
@@ -76,34 +85,44 @@
     here = strip(True, 0)
 
     for i in range(4):
-        plan(("l2", i), x_ref.at[:, part(sent_as[i])], cols.at[x, 1, :, part(sent_as[i])], shot_pair)
+        for p in (0, 1):
+            there = cols.at[x, 1, p, part(sent_as[i])]
+            plan(("l2", i, p), x_ref.at[p, part(sent_as[i])], there, shot_pair)
     for q in (0, 1):
-        plan(("zo", q), x_ref.at[:, part(there_part[q])], rows.at[q, 1, :, here], other_half)
-        plan(("zr", q), cols.at[x, 1, :, part(there_part[q])], rows.at[q, 0, :, here], other_half)
+        for p in (0, 1):
+            plan(("zo", q, p), x_ref.at[p, part(there_part[q])], rows.at[q, 1, p, here], other_half)
+            plan(("zr", q, p), cols.at[x, 1, p, part(there_part[q])], rows.at[q, 0, p, here], other_half)
     for s in (1, -1):
-        p = 0 if s == 1 else 1
-        plan(("xd", 0, s, 0), x_ref, cols.at[x, 0], xdev[s])
-        spot = cols.at[xs[-s], 0, p]
+        handed = 0 if s == 1 else 1
+        for p in (0, 1):
+            plan(("xd", 0, s, p), x_ref.at[p], cols.at[x, 0, p], xdev[s])
+        spot = cols.at[xs[-s], 0, handed]
         plan(("xf", 0, s, 0), spot, spot, xdev[s])
         for i in range(4):
             spot = cols.at[x, 1, :, part(order[i])]
             plan(("xd", 1, s, i), spot, spot, xdev[s])
-            spot = cols.at[xs[-s], 1, p, part(order[i])]
+            spot = cols.at[xs[-s], 1, handed, part(order[i])]
             plan(("xf", 1, s, i), spot, spot, xdev[s])
+
+    def source(zown, g, q, p):
+        if not zown:
+            return rows.at[q, g, p, strip(zown, 0)]
+        return x_ref.at[p, part(row_part[q])] if g == 0 else cols.at[x, 1, p, part(row_part[q])]
+
     for zown in (True, False):
         for g in (0, 1):
             for q in (0, 1):
-                spot = rows.at[q, g, :, strip(zown, 0)]
-                src = spot
-                if zown:
-                    src = x_ref.at[:, part(row_part[q])] if g == 0 else cols.at[x, 1, :, part(row_part[q])]
                 for s in (1, -1):
+                    for p in (0, 1):
+                        spot = rows.at[q, g, p, strip(zown, 0)]
+                        plan(("yd", zown, g, q, s, p), source(zown, g, q, p), spot, ydev[s])
                     p = 0 if s == 1 else 1
-                    plan(("yd", zown, g, q, s), src, spot, ydev[s])
-                    forward = rows.at[q, g, p, strip(zown, -s)]
-                    plan(("yf", zown, g, q, s), forward, forward, ydev[s])
-                plan(("cc", zown, g, q, 0), src, spot, sibling)
-                for yy in (1, -1, 2):
+                    spot = rows.at[q, g, p, strip(zown, -s)]
+                    plan(("yf", zown, g, q, s), spot, spot, ydev[s])
+                    spot = rows.at[q, g, p, strip(zown, 2)]
+                    plan(("cc", zown, g, q, 2, p), spot, spot, sibling)
+                plan(("cc", zown, g, q, 0), source(zown, g, q, slice(None)), rows.at[q, g, :, strip(zown, 0)], sibling)
+                for yy in (1, -1):
                     spot = rows.at[q, g, :, strip(zown, yy)]
                     plan(("cc", zown, g, q, yy), spot, spot, sibling)
 
@@ -117,26 +136,31 @@
         for q in (0, 1)
     }
 
-    def y_send(zown, g, q):
-        go(("yd", zown, g, q, 1), ("yd", zown, g, q, -1), ("cc", zown, g, q, 0))
+    def y_send(zown, g, q, p):
+        go(("yd", zown, g, q, 1, p), ("yd", zown, g, q, -1, p))
+        if p == 1:
+            go(("cc", zown, g, q, 0))
 
     def y_forward(zown, g, q):
         for s in (1, -1):
-            got(("yd", zown, g, q, s))
+            got(("yd", zown, g, q, s, 0 if s == 1 else 1))
             go(("yf", zown, g, q, s))
-        go(("cc", zown, g, q, 1), ("cc", zown, g, q, -1))
+        for s in (1, -1):
+            got(("yd", zown, g, q, s, 1 if s == 1 else 0))
+            go(("cc", zown, g, q, -s))
 
     def y_last(zown, g, q):
-        got(("yf", zown, g, q, 1), ("yf", zown, g, q, -1))
-        go(("cc", zown, g, q, 2))
-
-    def x_send(g, i):
-        go(("xd", g, 1, i), ("xd", g, -1, i))
-
-    def x_forward(g, i):
         for s in (1, -1):
-            got(("xd", g, s, i))
-            go(("xf", g, s, i))
+            got(("yf", zown, g, q, s))
+            go(("cc", zown, g, q, 2, 0 if s == 1 else 1))
+
+    def x_send(i):
+        go(("xd", 1, 1, i), ("xd", 1, -1, i))
+
+    def x_forward(i):
+        for s in (1, -1):
+            got(("xd", 1, s, i))
+            go(("xf", 1, s, i))
 
     def build(d, g, real, imag):
         w[d, g, 0, 0:ROWS] = real
@@ -149,68 +173,95 @@
 
     def take_sibling(zown, q):
         for g in (0, 1):
-            for yy in (0, 1, -1, 2):
-                got(("cc", zown, g, q, yy))
-
-    go(("l2", 0), ("l2", 1), ("zo", 0))
-    y_send(True, 0, 0)
-    x_send(0, 0)
-    go(("l2", 2), ("l2", 3), ("zo", 1))
-    y_send(True, 0, 1)
+            got(*(("cc", zown, g, q, yy) for yy in (0, 1, -1)))
+            got(("cc", zown, g, q, 2, 0), ("cc", zown, g, q, 2, 1))
+
+    go(*(("l2", i, p) for i in (0, 1) for p in (0, 1)))
+
+    @pl.when(zhi == 1)
+    def _():
+        go(("zo", 0, 0), ("zo", 0, 1))
+
+    for p in (0, 1):
+        y_send(True, 0, 0, p)
+    go(("xd", 0, 1, 0), ("xd", 0, -1, 1), ("xd", 0, 1, 1), ("xd", 0, -1, 0))
+    go(*(("l2", i, p) for i in (2, 3) for p in (0, 1)))
+    for p in (0, 1):
+        y_send(True, 0, 1, p)
+    mine_copy = pltpu.make_async_copy(x_ref, mine, lsem.at[4])
+    mine_copy.start()
     own[0, 0].start()
     own[0, 1].start()
-    build(0, 0, x_ref[0], x_ref[1])
+    mine_copy.wait()
+    build(0, 0, mine[0], mine[1])
 
     y_forward(True, 0, 0)
-    got(("zo", 0))
-    y_send(False, 1, 0)
-    got(("l2", 0))
-    go(("zr", 0))
-    x_send(1, 0)
+
+    @pl.when(zhi == 0)
+    def _():
+        pl.semaphore_wait(ready, 1)
+        go(("zo", 0, 0), ("zo", 0, 1))
+
+    for p in (0, 1):
+        got(("zo", 0, p))
+        y_send(False, 1, 0, p)
+    for p in (0, 1):
+        got(("l2", 0, p))
+        go(("zr", 0, p))
+    go(("zo", 1, 0), ("zo", 1, 1))
+    x_send(0)
     y_forward(False, 1, 0)
     y_last(True, 0, 0)
-    got(("l2", 1))
-    y_send(True, 1, 0)
+    for p in (0, 1):
+        got(("l2", 1, p))
+        y_send(True, 1, 0, p)
     own[1, 0].start()
-    x_send(1, 1)
-    got(("zr", 0))
-    y_send(False, 0, 0)
-    x_forward(0, 0)
+    x_send(1)
+    for p in (0, 1):
+        got(("zr", 0, p))
+        y_send(False, 0, 0, p)
+    got(("xd", 0, 1, 0), ("xd", 0, -1, 1))
+    go(("xf", 0, 1, 0), ("xf", 0, -1, 0))
     y_last(False, 1, 0)
     y_forward(True, 1, 0)
+    got(("xd", 0, 1, 1), ("xd", 0, -1, 0))
     build_from(1, 0, xs[1])
-    got(("l2", 2))
-    go(("zr", 1))
-    x_send(1, 2)
     y_forward(False, 0, 0)
+    for p in (0, 1):
+        got(("l2", 2, p))
+        go(("zr", 1, p))
+    x_send(2)
+    y_last(True, 1, 0)
     y_forward(True, 0, 1)
-    got(("zo", 1))
-    y_send(False, 1, 1)
-    y_last(True, 1, 0)
-    x_forward(1, 0)
-    x_forward(1, 1)
+    for p in (0, 1):
+        got(("zo", 1, p))
+        y_send(False, 1, 1, p)
+    x_forward(0)
+    x_forward(1)
+    build_from(2, 0, xs[-1])
     y_last(False, 0, 0)
-    build_from(2, 0, xs[-1])
-    got(("l2", 3))
-    y_send(True, 1, 1)
+    for p in (0, 1):
+        got(("l2", 3, p))
+        y_send(True, 1, 1, p)
     own[1, 1].start()
-    x_send(1, 3)
+    x_send(3)
     build_from(0, 1, x)
-    y_last(True, 0, 1)
-    got(("zr", 1))
-    y_send(False, 0, 1)
     own[0, 0].wait()
     own[1, 0].wait()
     take_sibling(True, 0)
 
     def before_1():
+        y_last(True, 0, 1)
+        for p in (0, 1):
+            got(("zr", 1, p))
+            y_send(False, 0, 1, p)
         take_sibling(False, 0)
         y_forward(False, 1, 1)
 
     def before_2():
         y_forward(True, 1, 1)
-        x_forward(1, 2)
-        x_forward(1, 3)
+        x_forward(2)
+        x_forward(3)
         build_from(1, 1, xs[1])
 
     def before_3():
@@ -298,6 +349,9 @@
 
     lax.fori_loop(0, 4, keep, 0)
 
+    for copy in msgs.values():
+        copy.wait_send()
+
     def finish(i, _):
         for copy in sums(i):
             copy.wait_recv()
@@ -320,9 +374,6 @@
 
     lax.fori_loop(0, 8, finish, 0)
 
-    for copy in msgs.values():
-        copy.wait_send()
-
     def drain(i, _):
         for copy in sums(i):
             copy.wait_send()
@@ -335,7 +386,7 @@
     flat = pl.pallas_call(
         kernel,
         out_shape=pltpu.VMEM((4096, 128), jnp.float32),
-        in_specs=[pl.BlockSpec(memory_space=pltpu.VMEM)],
+        in_specs=[pl.BlockSpec(memory_space=pltpu.HBM)],
         out_specs=pl.BlockSpec(memory_space=pltpu.VMEM),
         scratch_shapes=[
             pltpu.VMEM((4, 2, 2, ROWS, SHOTS), jnp.bfloat16),
@@ -349,10 +400,12 @@
             pltpu.VMEM((8, 8, WIDE), jnp.float32),
             pltpu.SemaphoreType.DMA((N_SEMS,)),
             pltpu.SemaphoreType.DMA((N_SEMS,)),
-            pltpu.SemaphoreType.DMA((4,)),
+            pltpu.SemaphoreType.DMA((5,)),
+            pltpu.SemaphoreType.REGULAR,
+            pltpu.VMEM((2, ROWS, SHOTS), jnp.bfloat16),
         ],
         compiler_params=pltpu.CompilerParams(
-            collective_id=0, has_side_effects=True, vmem_limit_bytes=52 * 2**20
+            collective_id=0, has_side_effects=True, vmem_limit_bytes=60 * 2**20
         ),
         cost_estimate=pl.CostEstimate(flops=8_600_000_000, bytes_accessed=3_000_000, transcendentals=1_000_000),
     )(records)

time: 68.8 us -> 67 us (0.974)
  Pallas kernels: 66.8 us -> 64.7 us
    pallas_call x1, Pallas kernels: 66.8 us -> 64.7 us  [on_device(): pl.pallas_call(kernel, out_shape=pltpu.VMEM((4096, 128), jnp.float32), in...]
where the time goes in v3:
time: 67 us; the launch traced here: 66.1 us
  Pallas kernels  64.7 us (97%)
  local copies, waits for them, and re-layouts  1.32 us (2%)
    pallas_call x1, Pallas kernels, on_device(): pl.pallas_call(kernel, out_shape=pltpu.VMEM((4096, 128), jnp.float32), in...  64.7 us

profile of v3, /device:TPU:16, one launch (start us, length us, event | category | flops | bytes accessed | tf_op | source)
XLA Modules:
  0.0 66.1 jit_solution(3287003815198579130)
XLA Ops:
  0.0 64.7 %shard_map.17 = f32[4096,128]{1,0:T(8,128)S(1)} custom-call(bf16[2,128,1024]{2,1,0:T(8,128)(2,1)} %x_ref.1), custom_call_target="tpu_custom_call" | custom-call | flops 8600000512 | bytes 3000000 | tf_op jit(solution)/shard_map/pallas_call | solution.py:386
  64.7 1.3 %copy.4 = f32[2,1,16,1,32,4,128]{6,5,4,3,2,1,0:T(4,128)} copy(f32[2,1,16,1,32,4,128]{6,5,4,3,2,1,0:T(4,128)S(1)} %bitcast.3) | data formatting | bytes 4194304

commit v4 on v3

--- a/solution.py
+++ b/solution.py
@@ -212,6 +212,8 @@
     x_send(0)
     y_forward(False, 1, 0)
     y_last(True, 0, 0)
+    got(("xd", 0, 1, 0), ("xd", 0, -1, 1))
+    go(("xf", 0, 1, 0), ("xf", 0, -1, 0))
     for p in (0, 1):
         got(("l2", 1, p))
         y_send(True, 1, 0, p)
@@ -220,8 +222,6 @@
     for p in (0, 1):
         got(("zr", 0, p))
         y_send(False, 0, 0, p)
-    got(("xd", 0, 1, 0), ("xd", 0, -1, 1))
-    go(("xf", 0, 1, 0), ("xf", 0, -1, 0))
     y_last(False, 1, 0)
     y_forward(True, 1, 0)
     got(("xd", 0, 1, 1), ("xd", 0, -1, 0))
@@ -239,7 +239,6 @@
     x_forward(0)
     x_forward(1)
     build_from(2, 0, xs[-1])
-    y_last(False, 0, 0)
     for p in (0, 1):
         got(("l2", 3, p))
         y_send(True, 1, 1, p)
@@ -251,6 +250,7 @@
     take_sibling(True, 0)
 
     def before_1():
+        y_last(False, 0, 0)
         y_last(True, 0, 1)
         for p in (0, 1):
             got(("zr", 1, p))
@@ -266,14 +266,12 @@
 
     def before_3():
         y_forward(False, 0, 1)
+
+    def before_4():
+        build_from(2, 1, xs[-1])
+
+    def before_5():
         y_last(False, 1, 1)
-
-    def before_4():
-        y_last(True, 1, 1)
-        build_from(2, 1, xs[-1])
-
-    def before_5():
-        y_last(False, 0, 1)
 
     def before_6():
         for s in (1, -1):
@@ -319,7 +317,7 @@
 
         top = lax.fori_loop(0, 4, look, jnp.zeros((8, WIDE), jnp.float32)).max(axis=0, keepdims=True)
         top = jnp.maximum(top, TINY)
-        top_out[i] = jnp.broadcast_to(top, (8, WIDE))
+        top_out[i] = top
         scale = PEAK / top
 
         def code(r, _):
@@ -338,6 +336,8 @@
 
     lax.fori_loop(0, 8, give, 0)
 
+    y_last(True, 1, 1)
+    y_last(False, 0, 1)
     own[0, 1].wait()
     own[1, 1].wait()
     take_sibling(True, 1)
@@ -358,7 +358,7 @@
         d = i // 2
         half = jnp.where(i % 2 == 0, zhi, 1 - zhi)
         xi = (x + d + (d // 2) * (1 - 2 * (d % 2))) % 4
-        top = top_in[i][0:1] * (1.0 / PEAK)
+        top = top_in[i] * (1.0 / PEAK)
 
         def add(r, _):
             u = enc_in[i, pl.ds(pl.multiple_of(r * 64, 64), 64)].astype(jnp.float32)
@@ -396,8 +396,8 @@
             pltpu.VMEM((4, 2 * HALF, WIDE), jnp.float32),
             pltpu.VMEM((8, HALF, WIDE), jnp.bfloat16),
             pltpu.VMEM((8, HALF, WIDE), jnp.bfloat16),
-            pltpu.VMEM((8, 8, WIDE), jnp.float32),
-            pltpu.VMEM((8, 8, WIDE), jnp.float32),
+            pltpu.VMEM((8, 1, WIDE), jnp.float32),
+            pltpu.VMEM((8, 1, WIDE), jnp.float32),
             pltpu.SemaphoreType.DMA((N_SEMS,)),
             pltpu.SemaphoreType.DMA((N_SEMS,)),
             pltpu.SemaphoreType.DMA((5,)),

time: 67 us -> 65.6 us (0.979)
  Pallas kernels: 64.7 us -> 63.7 us
    pallas_call x1, Pallas kernels: 64.7 us -> 63.7 us  [on_device(): pl.pallas_call(kernel, out_shape=pltpu.VMEM((4096, 128), jnp.float32), in...]
where the time goes in v4:
time: 65.6 us; the launch traced here: 65 us
  Pallas kernels  63.7 us (97%)
  local copies, waits for them, and re-layouts  1.32 us (2%)
    pallas_call x1, Pallas kernels, on_device(): pl.pallas_call(kernel, out_shape=pltpu.VMEM((4096, 128), jnp.float32), in...  63.7 us
    unnamed x1, local copies, waits for them, and re-layouts  1.32 us

profile of v4, /device:TPU:16, one launch (start us, length us, event | category | flops | bytes accessed | tf_op | source)
XLA Modules:
  0.0 65.0 jit_solution(16684871300474067694)
XLA Ops:
  0.0 63.7 %shard_map.17 = f32[4096,128]{1,0:T(8,128)S(1)} custom-call(bf16[2,128,1024]{2,1,0:T(8,128)(2,1)} %x_ref.1), custom_call_target="tpu_custom_call" | custom-call | flops 8600000512 | bytes 3000000 | tf_op jit(solution)/shard_map/pallas_call | solution.py:386
  63.7 1.3 %copy.4 = f32[2,1,16,1,32,4,128]{6,5,4,3,2,1,0:T(4,128)} copy(f32[2,1,16,1,32,4,128]{6,5,4,3,2,1,0:T(4,128)S(1)} %bitcast.3) | data formatting | bytes 4194304

commit v5 on v4

--- a/solution.py
+++ b/solution.py
@@ -185,7 +185,11 @@
     for p in (0, 1):
         y_send(True, 0, 0, p)
     go(("xd", 0, 1, 0), ("xd", 0, -1, 1), ("xd", 0, 1, 1), ("xd", 0, -1, 0))
-    go(*(("l2", i, p) for i in (2, 3) for p in (0, 1)))
+
+    @pl.when(c == 0)
+    def _():
+        go(*(("l2", i, p) for i in (2, 3) for p in (0, 1)))
+
     for p in (0, 1):
         y_send(True, 0, 1, p)
     mine_copy = pltpu.make_async_copy(x_ref, mine, lsem.at[4])
@@ -196,6 +200,11 @@
     build(0, 0, mine[0], mine[1])
 
     y_forward(True, 0, 0)
+
+    @pl.when(c == 1)
+    def _():
+        go(*(("l2", i, p) for i in (2, 3) for p in (0, 1)))
+
 
     @pl.when(zhi == 0)
     def _():
@@ -315,7 +324,7 @@
         def look(r, top):
             return jnp.maximum(top, jnp.abs(acc0[pl.ds(pl.multiple_of(r * 64, 64), 64)]).reshape(8, 8, WIDE).max(axis=0))
 
-        top = lax.fori_loop(0, 4, look, jnp.zeros((8, WIDE), jnp.float32)).max(axis=0, keepdims=True)
+        top = lax.fori_loop(0, 4, look, jnp.zeros((8, WIDE), jnp.float32), unroll=True).max(axis=0, keepdims=True)
         top = jnp.maximum(top, TINY)
         top_out[i] = top
         scale = PEAK / top
@@ -329,7 +338,7 @@
             enc_out[i, at] = jnp.where(t < 0, -power, power).astype(jnp.bfloat16)
             return 0
 
-        lax.fori_loop(0, 4, code, 0)
+        lax.fori_loop(0, 4, code, 0, unroll=True)
         for copy in sums(i):
             copy.start()
         return 0
@@ -369,7 +378,7 @@
                 o_ref[pl.ds(k * 2048 + r * 512 + half * 256 + xi, 64, stride=4), :] = total[:, k * ROWS : (k + 1) * ROWS]
             return 0
 
-        lax.fori_loop(0, 4, add, 0)
+        lax.fori_loop(0, 4, add, 0, unroll=True)
         return 0
 
     lax.fori_loop(0, 8, finish, 0)

time: 65.6 us -> 65.5 us (level)
  no operation moved by 1% of the time
where the time goes in v5:
time: 65.5 us; the launch traced here: 64.9 us
  Pallas kernels  63.6 us (97%)
  local copies, waits for them, and re-layouts  1.32 us (2%)
    pallas_call x1, Pallas kernels, on_device(): pl.pallas_call(kernel, out_shape=pltpu.VMEM((4096, 128), jnp.float32), in...  63.6 us
    unnamed x1, local copies, waits for them, and re-layouts  1.32 us

profile of v5, /device:TPU:16, one launch (start us, length us, event | category | flops | bytes accessed | tf_op | source)
XLA Modules:
  0.0 64.9 jit_solution(10355401877872385106)
XLA Ops:
  0.0 63.6 %shard_map.17 = f32[4096,128]{1,0:T(8,128)S(1)} custom-call(bf16[2,128,1024]{2,1,0:T(8,128)(2,1)} %x_ref.1), custom_call_target="tpu_custom_call" | custom-call | flops 8600000512 | bytes 3000000 | tf_op jit(solution)/shard_map/pallas_call | solution.py:395
  63.6 1.3 %copy.4 = f32[2,1,16,1,32,4,128]{6,5,4,3,2,1,0:T(4,128)} copy(f32[2,1,16,1,32,4,128]{6,5,4,3,2,1,0:T(4,128)S(1)} %bitcast.3) | data formatting | bytes 4194304

commit v6 on v5

--- a/solution.py
+++ b/solution.py
@@ -221,6 +221,7 @@
     x_send(0)
     y_forward(False, 1, 0)
     y_last(True, 0, 0)
+    y_forward(True, 0, 1)
     got(("xd", 0, 1, 0), ("xd", 0, -1, 1))
     go(("xf", 0, 1, 0), ("xf", 0, -1, 0))
     for p in (0, 1):
@@ -241,7 +242,6 @@
         go(("zr", 1, p))
     x_send(2)
     y_last(True, 1, 0)
-    y_forward(True, 0, 1)
     for p in (0, 1):
         got(("zo", 1, p))
         y_send(False, 1, 1, p)

time: 65.5 us -> 65.7 us (level)
  Pallas kernels: 63.6 us -> 64.3 us
    pallas_call x1, Pallas kernels: 63.6 us -> 64.3 us  [on_device(): pl.pallas_call(kernel, out_shape=pltpu.VMEM((4096, 128), jnp.float32), in...]
where the time goes in v6:
time: 65.7 us
  Pallas kernels  64.3 us (98%)
  local copies, waits for them, and re-layouts  1.32 us (2%)
    pallas_call x1, Pallas kernels, on_device(): pl.pallas_call(kernel, out_shape=pltpu.VMEM((4096, 128), jnp.float32), in...  64.3 us
    unnamed x1, local copies, waits for them, and re-layouts  1.32 us

profile of v6, /device:TPU:16, one launch (start us, length us, event | category | flops | bytes accessed | tf_op | source)
XLA Modules:
  0.0 65.7 jit_solution(1235916772808102026)
XLA Ops:
  0.0 64.3 %shard_map.17 = f32[4096,128]{1,0:T(8,128)S(1)} custom-call(bf16[2,128,1024]{2,1,0:T(8,128)(2,1)} %x_ref.1), custom_call_target="tpu_custom_call" | custom-call | flops 8600000512 | bytes 3000000 | tf_op jit(solution)/shard_map/pallas_call | solution.py:395
  64.3 1.3 %copy.4 = f32[2,1,16,1,32,4,128]{6,5,4,3,2,1,0:T(4,128)} copy(f32[2,1,16,1,32,4,128]{6,5,4,3,2,1,0:T(4,128)S(1)} %bitcast.3) | data formatting | bytes 4194304
